TPU v7x, 32 devices: a whole 2x2x4 slice. The times are simulated.
32 devices in a mesh: radial: 8 (over y, x, core), axial: 4 (over z).
Axes of the slice: x: 2, y: 2, z: 4, core: 2. Of those that a mesh axis runs over, the one named last changes fastest.
Arguments:
- rhs: float32 [2, 2, 96, 64, 512], P(None, None, None, 'radial', 'axial'), may hold values from -6 to 6
- mat_ids: int32 [96, 64, 512], P(None, 'radial', 'axial'), may hold values from 0 to 3
- stiff_table: float32 [4], replicated, may hold values from 0.5 to 4
- dens_table: float32 [4], replicated, may hold values from 0.5 to 2
- mass_shift: float32 [2], replicated, may hold values from 0.5 to 2
- harmonic: int32 [2], replicated, may hold values from 1 to 12
- radial_factor: float32 [2, 2, 16, 16], replicated, may hold values from -0.09375 to 0.09375
- axial_factor: float32 [2, 2, 64, 64], replicated, may hold values from -0.046875 to 0.046875
Outputs:
- solution: float32 [2, 2, 96, 64, 512], P(None, None, None, 'radial', 'axial')
- residual: float32 [2, 2, 96, 64, 512], P(None, None, None, 'radial', 'axial')
All inputs are finite; a program needn't handle non-finite values.
Results may differ from a plain program's by a relative error of at most 0.00021.
Values sent between devices are 32-bit elements; how exact they have to be, the bound alone decides.
A program may use at most 128 MiB of HBM per device.

v0:
```python
import jax
import jax.numpy as jnp
from jax import lax
from jax.sharding import PartitionSpec as P

ITERS = 3
NSECT = 24
AR = 4
AA = 8
LOSS_FACTOR = 0.2
RELAXATION = 0.6


def extended(shard, sides, width):
    for axis, dim in sides:
        size, length = (lax.axis_size(axis), shard.shape[dim])
        up = [(i, (i + 1) % size) for i in range(size - 1)]
        down = [(j, i) for i, j in up]
        last = lax.slice_in_dim(shard, length - width, length, axis=dim)
        first = lax.slice_in_dim(shard, 0, width, axis=dim)
        before = lax.ppermute(last, axis, up)
        after = lax.ppermute(first, axis, down)
        shard = jnp.concatenate([before, shard, after], axis=dim)
    return shard


def material(mat_ids, table):
    result = jnp.zeros(mat_ids.shape, table.dtype)
    for entry in range(table.shape[0]):
        result = result + jnp.where(mat_ids == entry, table[entry], jnp.zeros((), table.dtype))
    return result


def couplings(stiffness, padded):
    return (
        0.5 * (stiffness + padded[:, 2:, 1:-1]),
        0.5 * (stiffness + padded[:, :-2, 1:-1]),
        0.5 * (stiffness + padded[:, 1:-1, 2:]),
        0.5 * (stiffness + padded[:, 1:-1, :-2]),
        0.5 * (stiffness + jnp.roll(stiffness, -1, 0)),
        0.5 * (stiffness + jnp.roll(stiffness, 1, 0)),
    )


def neighbours(values, padded, weights, cosines, sines):
    summed = weights[0] * padded[:, :, :, 2:, 1:-1] + weights[1] * padded[:, :, :, :-2, 1:-1]
    summed = (
        summed + weights[2] * padded[:, :, :, 1:-1, 2:] + weights[3] * padded[:, :, :, 1:-1, :-2]
    )
    real_part = values[0]
    imag_part = values[1]
    cosine = cosines[:, None, None, None]
    sine = sines[:, None, None, None]
    wrap_real = cosine * real_part[:, :1] - sine * imag_part[:, :1]
    wrap_imag = sine * real_part[:, :1] + cosine * imag_part[:, :1]
    ahead = jnp.stack(
        [
            jnp.concatenate([real_part[:, 1:], wrap_real], 1),
            jnp.concatenate([imag_part[:, 1:], wrap_imag], 1),
        ]
    )
    back_real = cosine * real_part[:, -1:] + sine * imag_part[:, -1:]
    back_imag = cosine * imag_part[:, -1:] - sine * real_part[:, -1:]
    behind = jnp.stack(
        [
            jnp.concatenate([back_real, real_part[:, :-1]], 1),
            jnp.concatenate([back_imag, imag_part[:, :-1]], 1),
        ]
    )
    return summed + weights[4] * ahead + weights[5] * behind


def operate(values, weights, diag_real, diag_imag, cosines, sines):
    padded = extended(values, (("radial", 3), ("axial", 4)), 1)
    coupled = neighbours(values, padded, weights, cosines, sines)
    real_out = (
        diag_real * values[0] - diag_imag * values[1] - (coupled[0] - LOSS_FACTOR * coupled[1])
    )
    imag_out = (
        diag_real * values[1] + diag_imag * values[0] - (coupled[1] + LOSS_FACTOR * coupled[0])
    )
    return jnp.stack([real_out, imag_out])


def right_product(left_real, left_imag, right_real, right_imag):

    def matmul(first, second):
        return jnp.einsum("hij,hkj->hik", first, second, precision=lax.Precision.HIGHEST)

    return (
        matmul(left_real, right_real) - matmul(left_imag, right_imag),
        matmul(left_real, right_imag) + matmul(left_imag, right_real),
    )


def left_product(left_real, left_imag, right_real, right_imag):

    def matmul(first, second):
        return jnp.einsum("hij,hjk->hik", first, second, precision=lax.Precision.HIGHEST)

    return (
        matmul(left_real, right_real) - matmul(left_imag, right_imag),
        matmul(left_real, right_imag) + matmul(left_imag, right_real),
    )


def jacobi_step(residual, diag_real, diag_imag):
    scale = RELAXATION / (diag_real * diag_real + diag_imag * diag_imag)
    real_out = (diag_real * residual[0] + diag_imag * residual[1]) * scale
    imag_out = (diag_real * residual[1] - diag_imag * residual[0]) * scale
    return jnp.stack([real_out, imag_out])


def coarse_correction(residual, radial_factor, axial_factor):
    shape = residual.shape
    band_rows = shape[3] // AR
    band_cols = shape[4] // AA
    blocks = residual.reshape(2, shape[1], shape[2], band_rows, AR, band_cols, AA)
    coarse_res = jnp.sum(blocks, axis=(2, 4, 6))
    mine_axial = lax.dynamic_slice_in_dim(
        axial_factor, lax.axis_index("axial") * band_cols, band_cols, 2
    )
    mine_radial = lax.dynamic_slice_in_dim(
        radial_factor, lax.axis_index("radial") * band_rows, band_rows, 2
    )
    radial_count = lax.axis_size("radial")
    axial_count = lax.axis_size("axial")
    collected = lax.all_gather(coarse_res[None], ("radial", "axial"), axis=0, tiled=True)
    collected = collected.reshape(radial_count, axial_count, 2, shape[1], band_rows, band_cols)
    collected = collected.transpose(2, 3, 0, 4, 1, 5).reshape(
        2, shape[1], radial_count * band_rows, axial_count * band_cols
    )
    mixed_real, mixed_imag = right_product(collected[0], collected[1], mine_axial[0], mine_axial[1])
    corr_real, corr_imag = left_product(mine_radial[0], mine_radial[1], mixed_real, mixed_imag)
    spread = jnp.repeat(jnp.repeat(jnp.stack([corr_real, corr_imag]), AR, axis=2), AA, axis=3)
    return spread[:, :, None]


def local(rhs, mat_ids, stiff_table, dens_table, mass_shift, harmonic, radial_factor, axial_factor):
    stiffness = material(mat_ids, stiff_table)
    density = material(mat_ids, dens_table)
    padded_stiff = extended(stiffness, (("radial", 1), ("axial", 2)), 1)
    weights = couplings(stiffness, padded_stiff)
    total = weights[0] + weights[1] + weights[2] + weights[3] + weights[4] + weights[5]
    diag_real = total[None] - mass_shift[:, None, None, None] * density[None]
    diag_imag = LOSS_FACTOR * total
    angles = 2.0 * jnp.pi / NSECT * harmonic.astype(jnp.float32)
    cosines = jnp.cos(angles)
    sines = jnp.sin(angles)
    solution = jnp.zeros_like(rhs)
    residual = rhs
    for iteration in range(ITERS):
        if iteration > 0:
            residual = rhs - operate(solution, weights, diag_real, diag_imag, cosines, sines)
        correction = coarse_correction(residual, radial_factor, axial_factor)
        solution = solution + jacobi_step(residual, diag_real, diag_imag) + correction
    residual = rhs - operate(solution, weights, diag_real, diag_imag, cosines, sines)
    return (solution, residual)


def solution(mesh):
    return jax.shard_map(
        local,
        mesh=mesh,
        in_specs=(
            P(None, None, None, "radial", "axial"),
            P(None, "radial", "axial"),
            P(),
            P(),
            P(),
            P(),
            P(),
            P(),
        ),
        out_specs=(P(None, None, None, "radial", "axial"), P(None, None, None, "radial", "axial")),
        check_vma=False,
    )
```

profile of v0, /device:TPU:12, one launch (start us, length us, event | category | flops | bytes accessed | tf_op | source)
XLA Modules:
  0.0 395.2 jit_solution(4183586601979156998)
XLA Ops:
  3.6 4.6 %select_add_fusion = (f32[96,8,128]{2,0,1:T(8,128)}, pred[96,8,128]{2,0,1:T(8,128)(4,1)S(1)}, pred[96,8,128]{2,0,1:T(8,128)(4,1)S(1)}, pred[96,8,128]{2,0,1:T(8,128)(4,1)S(1)}, pred[96,8,128]{2,0,1:T(8,128)(4,1)S(1)}) fusion(f32[]{:T(128)} %bitcast.7, f32[]{:T(128)} %bitcast.6, f32[]{:T(128)} %bitcast.5, f32[]{:T(128)} %bitcast.4, s32[96,8,128]{2,1,0:T(8,128)} %param.9), kind=kLoop, calls=%fused_computation.139 | loop fusion | flops 1081344 | bytes 1179664 | tf_op jit(solution)/shard_map/add | solution.py:30
  8.2 2.8 select_add_fusion.1
  13.0 4.5 %collective-permute-start = (f32[96,1,128]{2,0,1:T(8,128)S(1)}, f32[96,1,128]{2,0,1:T(8,128)S(1)}, u32[]{:S(2)}, u32[]{:S(2)}) collective-permute-start(f32[96,1,128]{2,0,1:T(8,128)S(1)} %get-tuple-element.85), channel_id=1, source_target_pairs={{4,0},{8,4},{12,8},{16,12},{20,16},{24,20},{28,24},{5,1},{9,5},{13... | collective-permute-start | bytes 147464 | tf_op jit(solution)/shard_map/ppermute | solution.py:22
  18.9 65.0 %all-gather = f32[64,2,2,16]{3,2,1,0:T(2,128)S(1)} all-gather(f32[2,2,2,16]{3,2,1,0:T(2,128)S(1)} %reduce_sum.38), channel_id=2, replica_groups=mesh['radial'=8,'axial'=4] {'radial','axial'}, dimensions={0}, use_global_device_ids=true | all-gather | bytes 16896 | tf_op jit(solution)/shard_map/all_gather | solution.py:128
  89.5 4.8 %collective-permute-start.2 = (f32[96,10,1]{0,1,2:T(8,128)S(1)}, f32[96,10,1]{0,1,2:T(8,128)S(1)}, u32[]{:S(2)}, u32[]{:S(2)}) collective-permute-start(f32[96,10,1]{0,1,2:T(8,128)S(1)} %copy.253), channel_id=1, source_target_pairs={{1,0},{2,1},{3,2},{5,4},{6,5},{7,6},{9,8},{10,9},{11,10},{13,12},{... | collective-permute-start | bytes 11528 | tf_op jit(solution)/shard_map/ppermute | solution.py:22
  101.1 2.9 broadcast_multiply_fusion
  109.0 2.4 collective-permute-start.5
  118.1 3.6 fusion.83
  126.0 3.0 copy.222
  129.0 4.2 %collective-permute-start.6 = (f32[2,2,96,10,1]{2,1,4,3,0:T(2,128)}, f32[2,2,96,10,1]{2,1,4,3,0:T(2,128)}, u32[]{:S(2)}, u32[]{:S(2)}) collective-permute-start(f32[2,2,96,10,1]{2,1,4,3,0:T(2,128)} %copy.222), channel_id=1, source_target_pairs={{1,0},{2,1},{3,2},{5,4},{6,5},{7,6},{9,8},{10,9},{11,10},{13,12},{... | collective-permute-start | bytes 46088 | tf_op jit(solution)/shard_map/ppermute | solution.py:22
  143.6 3.1 copy.223
  146.7 6.0 %fusion.21 = f32[2,2,96,8,128]{4,3,2,1,0:T(8,128)S(1)} fusion(f32[2,2,96,10,1]{4,3,2,1,0:T(8,128)} %copy.226, f32[2,2,96,1,128]{4,3,2,1,0:T(1,128)S(1)} %collective-permute-done.4, f32[2,2,96,8,128]{4,3,2,1,0:T(8,128)S(1)} %maximum_add_fusion, f32[2,2,96,1,128]{4,3,2,1,0:T(1,128)} %copy-done.32, f32[2,2,96,10,1]{4,3,2,1,0:T(8,128)} %copy.223, ...), kind=kLoop, calls=%fused_computation.41 | loop fusion | flops 8257536 | bytes 9074688 | tf_op jit(solution)/shard_map/add | solution.py:70
  157.4 64.0 %all-gather.1 = f32[64,2,2,16]{3,2,1,0:T(2,128)S(1)} all-gather(f32[2,2,2,16]{3,2,1,0:T(2,128)S(1)} %copy.250), channel_id=3, replica_groups=mesh['radial'=8,'axial'=4] {'radial','axial'}, dimensions={0}, use_global_device_ids=true | all-gather | bytes 16896 | tf_op jit(solution)/shard_map/all_gather | solution.py:128
  221.9 3.0 add_multiply_fusion.1
  234.5 2.4 collective-permute-start.9
  239.7 2.7 collective-permute-done.9
  243.6 3.6 fusion.82
  251.5 3.0 copy.234
  254.5 4.1 %collective-permute-start.10 = (f32[2,2,96,10,1]{2,1,4,3,0:T(2,128)}, f32[2,2,96,10,1]{2,1,4,3,0:T(2,128)}, u32[]{:S(2)}, u32[]{:S(2)}) collective-permute-start(f32[2,2,96,10,1]{2,1,4,3,0:T(2,128)} %copy.234), channel_id=1, source_target_pairs={{1,0},{2,1},{3,2},{5,4},{6,5},{7,6},{9,8},{10,9},{11,10},{13,12},{... | collective-permute-start | bytes 46088 | tf_op jit(solution)/shard_map/ppermute | solution.py:22
  263.1 3.1 copy.235
  266.2 6.0 %fusion.12 = f32[2,2,96,8,128]{4,3,2,1,0:T(8,128)S(1)} fusion(f32[2,2,96,10,1]{4,3,2,1,0:T(8,128)} %copy.237, f32[2,2,96,1,128]{4,3,2,1,0:T(1,128)S(1)} %collective-permute-done.8, f32[2,2,96,8,128]{4,3,2,1,0:T(8,128)S(1)} %fusion.27, f32[2,2,96,1,128]{4,3,2,1,0:T(1,128)} %copy-done.34, f32[2,2,96,10,1]{4,3,2,1,0:T(8,128)} %copy.235, ...), kind=kLoop, calls=%fused_computation.24 | loop fusion | flops 8257536 | bytes 9074688 | tf_op jit(solution)/shard_map/add | solution.py:70
  276.9 64.0 %all-gather.2 = f32[64,2,2,16]{3,2,1,0:T(2,128)S(1)} all-gather(f32[2,2,2,16]{3,2,1,0:T(2,128)S(1)} %copy.252), channel_id=4, replica_groups=mesh['radial'=8,'axial'=4] {'radial','axial'}, dimensions={0}, use_global_device_ids=true | all-gather | bytes 16896 | tf_op jit(solution)/shard_map/all_gather | solution.py:128
  341.4 3.0 add_multiply_fusion
  348.5 2.6 fusion.28
  355.1 2.4 collective-permute-start.13
  360.4 2.6 collective-permute-done.13
  364.3 3.6 fusion.81
  367.9 2.6 copy.245
  372.4 3.2 copy.243
  375.6 4.2 %collective-permute-start.14 = (f32[2,2,96,10,1]{2,3,4,1,0:T(8,128)}, f32[2,2,96,10,1]{2,3,4,1,0:T(8,128)}, u32[]{:S(2)}, u32[]{:S(2)}) collective-permute-start(f32[2,2,96,10,1]{2,3,4,1,0:T(8,128)} %copy.243), channel_id=1, source_target_pairs={{1,0},{2,1},{3,2},{5,4},{6,5},{7,6},{9,8},{10,9},{11,10},{13,12},{... | collective-permute-start | bytes 46088 | tf_op jit(solution)/shard_map/ppermute | solution.py:22
  384.2 3.1 copy.244
  387.3 6.0 %fusion.3 = f32[2,2,96,8,128]{4,3,2,1,0:T(8,128)S(1)} fusion(f32[2,2,96,10,1]{4,3,2,1,0:T(8,128)} %copy.246, f32[2,2,96,1,128]{4,3,2,1,0:T(1,128)S(1)} %collective-permute-done.12, f32[2,2,96,8,128]{4,3,2,1,0:T(8,128)S(1)} %fusion.28, f32[2,2,96,1,128]{4,3,2,1,0:T(1,128)} %copy-done.33, f32[2,2,96,10,1]{4,3,2,1,0:T(8,128)} %copy.244, ...), kind=kLoop, calls=%fused_computation.7 | loop fusion | flops 8257536 | bytes 9074688 | tf_op jit(solution)/shard_map/add | solution.py:70
  (237 shorter events, 97.8 us)
Async XLA Ops:
  0.6 83.5 %copy-start = (f32[2,2,64,64]{3,2,1,0:T(8,128)S(1)}, f32[2,2,64,64]{3,2,1,0:T(8,128)}, u32[]{:S(2)}) copy-start(f32[2,2,64,64]{3,2,1,0:T(8,128)} %param.15) | copy-start | bytes 196612
  8.2 10.3 %copy-start.2 = (f32[2,2,96,8,128]{4,3,2,1,0:T(8,128)S(1)}, f32[2,2,96,8,128]{4,3,2,1,0:T(8,128)}, u32[]{:S(2)}) copy-start(f32[2,2,96,8,128]{4,3,2,1,0:T(8,128)} %param.8) | copy-start | bytes 4718596
  11.1 77.8 %collective-permute-start.1 = (f32[96,1,128]{2,0,1:T(8,128)S(1)}, f32[96,1,128]{2,0,1:T(8,128)S(1)}, u32[]{:S(2)}, u32[]{:S(2)}) collective-permute-start(f32[96,1,128]{2,0,1:T(8,128)S(1)} %get-tuple-element.86), channel_id=1, source_target_pairs={{0,4},{4,8},{8,12},{12,16},{16,20},{20,24},{24,28},{1,5},{5,9},{9,... | collective-permute-start | bytes 147464 | tf_op jit(solution)/shard_map/ppermute | solution.py:21
  13.0 75.9 %collective-permute-start = (f32[96,1,128]{2,0,1:T(8,128)S(1)}, f32[96,1,128]{2,0,1:T(8,128)S(1)}, u32[]{:S(2)}, u32[]{:S(2)}) collective-permute-start(f32[96,1,128]{2,0,1:T(8,128)S(1)} %get-tuple-element.85), channel_id=1, source_target_pairs={{4,0},{8,4},{12,8},{16,12},{20,16},{24,20},{28,24},{5,1},{9,5},{13... | collective-permute-start | bytes 147464 | tf_op jit(solution)/shard_map/ppermute | solution.py:22
  18.5 68.9 %copy-start.42 = (s32[2]{0:T(128)S(1)}, s32[2]{0:T(128)}, u32[]{:S(2)}) copy-start(s32[2]{0:T(128)} %param.13) | copy-start | bytes 28
  89.5 8.5 %collective-permute-start.2 = (f32[96,10,1]{0,1,2:T(8,128)S(1)}, f32[96,10,1]{0,1,2:T(8,128)S(1)}, u32[]{:S(2)}, u32[]{:S(2)}) collective-permute-start(f32[96,10,1]{0,1,2:T(8,128)S(1)} %copy.253), channel_id=1, source_target_pairs={{1,0},{2,1},{3,2},{5,4},{6,5},{7,6},{9,8},{10,9},{11,10},{13,12},{... | collective-permute-start | bytes 11528 | tf_op jit(solution)/shard_map/ppermute | solution.py:22
  94.5 5.7 %collective-permute-start.3 = (f32[96,10,1]{0,1,2:T(8,128)S(1)}, f32[96,10,1]{0,1,2:T(8,128)}, u32[]{:S(2)}, u32[]{:S(2)}) collective-permute-start(f32[96,10,1]{0,1,2:T(8,128)S(1)} %copy.254), channel_id=1, source_target_pairs={{0,1},{1,2},{2,3},{4,5},{5,6},{6,7},{8,9},{9,10},{10,11},{12,13},{... | collective-permute-start | bytes 11528 | tf_op jit(solution)/shard_map/ppermute | solution.py:21
  97.7 7.0 %copy-start.3 = (f32[96,8,128]{2,1,0:T(8,128)}, f32[96,8,128]{2,1,0:T(8,128)S(1)}, u32[]{:S(2)}) copy-start(f32[96,8,128]{2,1,0:T(8,128)S(1)} %copy.213) | copy-start | bytes 1179652
  107.0 8.4 %collective-permute-start.4 = (f32[2,2,96,1,128]{4,3,2,1,0:T(1,128)S(1)}, f32[2,2,96,1,128]{4,3,2,1,0:T(1,128)S(1)}, u32[]{:S(2)}, u32[]{:S(2)}) collective-permute-start(f32[2,2,96,1,128]{4,3,2,1,0:T(1,128)S(1)} %get-tuple-element.66), channel_id=1, source_target_pairs={{4,0},{8,4},{12,8},{16,12},{20,16},{24,20},{28,24},{5,1},{9,5},{13... | collective-permute-start | bytes 589832 | tf_op jit(solution)/shard_map/ppermute | solution.py:22
  109.0 7.9 %collective-permute-start.5 = (f32[2,2,96,1,128]{4,3,2,1,0:T(1,128)S(1)}, f32[2,2,96,1,128]{4,3,2,1,0:T(1,128)S(1)}, u32[]{:S(2)}, u32[]{:S(2)}) collective-permute-start(f32[2,2,96,1,128]{4,3,2,1,0:T(1,128)S(1)} %get-tuple-element.65), channel_id=1, source_target_pairs={{0,4},{4,8},{8,12},{12,16},{16,20},{20,24},{24,28},{1,5},{5,9},{9,... | collective-permute-start | bytes 589832 | tf_op jit(solution)/shard_map/ppermute | solution.py:21
  124.1 17.2 %collective-permute-start.7 = (f32[2,2,96,10,1]{2,1,4,3,0:T(2,128)S(1)}, f32[2,2,96,10,1]{2,1,4,3,0:T(2,128)S(1)}, u32[]{:S(2)}, u32[]{:S(2)}) collective-permute-start(f32[2,2,96,10,1]{2,1,4,3,0:T(2,128)S(1)} %copy.225), channel_id=1, source_target_pairs={{0,1},{1,2},{2,3},{4,5},{5,6},{6,7},{8,9},{9,10},{10,11},{12,13},{... | collective-permute-start | bytes 46088 | tf_op jit(solution)/shard_map/ppermute | solution.py:21
  129.0 6.4 %copy-start.31 = (f32[96,8,128]{2,0,1:T(8,128)S(1)}, f32[96,8,128]{2,0,1:T(8,128)}, u32[]{:S(2)}) copy-start(f32[96,8,128]{2,0,1:T(8,128)} %get-tuple-element.24) | copy-start | bytes 1179652
  129.0 7.3 %copy-start.30 = (f32[96,8,128]{2,0,1:T(8,128)S(1)}, f32[96,8,128]{2,0,1:T(8,128)}, u32[]{:S(2)}) copy-start(f32[96,8,128]{2,0,1:T(8,128)} %get-tuple-element.23) | copy-start | bytes 1179652
  129.0 14.7 %collective-permute-start.6 = (f32[2,2,96,10,1]{2,1,4,3,0:T(2,128)}, f32[2,2,96,10,1]{2,1,4,3,0:T(2,128)}, u32[]{:S(2)}, u32[]{:S(2)}) collective-permute-start(f32[2,2,96,10,1]{2,1,4,3,0:T(2,128)} %copy.222), channel_id=1, source_target_pairs={{1,0},{2,1},{3,2},{5,4},{6,5},{7,6},{9,8},{10,9},{11,10},{13,12},{... | collective-permute-start | bytes 46088 | tf_op jit(solution)/shard_map/ppermute | solution.py:22
  154.6 67.3 %copy-start.5 = (f32[96,8,128]{2,1,0:T(8,128)S(1)}, f32[96,8,128]{2,1,0:T(8,128)}, u32[]{:S(2)}) copy-start(f32[96,8,128]{2,1,0:T(8,128)} %copy-done.3) | copy-start | bytes 1179652
  154.6 67.3 %copy-start.11 = (f32[96,8,128]{2,1,0:T(8,128)S(1)}, f32[96,8,128]{2,1,0:T(8,128)}, u32[]{:S(2)}) copy-start(f32[96,8,128]{2,1,0:T(8,128)} %copy-done.9) | copy-start | bytes 1179652
  154.6 67.3 %copy-start.17 = (f32[96,8,128]{2,1,0:T(8,128)S(1)}, f32[96,8,128]{2,1,0:T(8,128)}, u32[]{:S(2)}) copy-start(f32[96,8,128]{2,1,0:T(8,128)} %copy-done.15) | copy-start | bytes 1179652
  154.6 67.4 %copy-start.24 = (f32[96,8,128]{2,1,0:T(8,128)S(1)}, f32[96,8,128]{2,1,0:T(8,128)}, u32[]{:S(2)}) copy-start(f32[96,8,128]{2,1,0:T(8,128)} %copy-done.23) | copy-start | bytes 1179652
  232.6 7.1 %collective-permute-start.8 = (f32[2,2,96,1,128]{4,3,2,1,0:T(1,128)S(1)}, f32[2,2,96,1,128]{4,3,2,1,0:T(1,128)S(1)}, u32[]{:S(2)}, u32[]{:S(2)}) collective-permute-start(f32[2,2,96,1,128]{4,3,2,1,0:T(1,128)S(1)} %get-tuple-element.62), channel_id=1, source_target_pairs={{4,0},{8,4},{12,8},{16,12},{20,16},{24,20},{28,24},{5,1},{9,5},{13... | collective-permute-start | bytes 589832 | tf_op jit(solution)/shard_map/ppermute | solution.py:22
  234.5 7.9 %collective-permute-start.9 = (f32[2,2,96,1,128]{4,3,2,1,0:T(1,128)S(1)}, f32[2,2,96,1,128]{4,3,2,1,0:T(1,128)S(1)}, u32[]{:S(2)}, u32[]{:S(2)}) collective-permute-start(f32[2,2,96,1,128]{4,3,2,1,0:T(1,128)S(1)} %get-tuple-element.61), channel_id=1, source_target_pairs={{0,4},{4,8},{8,12},{12,16},{16,20},{20,24},{24,28},{1,5},{5,9},{9,... | collective-permute-start | bytes 589832 | tf_op jit(solution)/shard_map/ppermute | solution.py:21
  249.6 11.1 %collective-permute-start.11 = (f32[2,2,96,10,1]{2,1,4,3,0:T(2,128)S(1)}, f32[2,2,96,10,1]{2,1,4,3,0:T(2,128)S(1)}, u32[]{:S(2)}, u32[]{:S(2)}) collective-permute-start(f32[2,2,96,10,1]{2,1,4,3,0:T(2,128)S(1)} %copy.236), channel_id=1, source_target_pairs={{0,1},{1,2},{2,3},{4,5},{5,6},{6,7},{8,9},{9,10},{10,11},{12,13},{... | collective-permute-start | bytes 46088 | tf_op jit(solution)/shard_map/ppermute | solution.py:21
  254.5 8.6 %collective-permute-start.10 = (f32[2,2,96,10,1]{2,1,4,3,0:T(2,128)}, f32[2,2,96,10,1]{2,1,4,3,0:T(2,128)}, u32[]{:S(2)}, u32[]{:S(2)}) collective-permute-start(f32[2,2,96,10,1]{2,1,4,3,0:T(2,128)} %copy.234), channel_id=1, source_target_pairs={{1,0},{2,1},{3,2},{5,4},{6,5},{7,6},{9,8},{10,9},{11,10},{13,12},{... | collective-permute-start | bytes 46088 | tf_op jit(solution)/shard_map/ppermute | solution.py:22
  266.2 6.0 %copy-start.37 = (f32[2]{0:T(128)S(1)}, f32[2]{0:T(128)}, u32[]{:S(2)}) copy-start(f32[2]{0:T(128)} %param.12) | copy-start | bytes 28
  274.0 67.3 %copy-start.7 = (f32[96,8,128]{2,1,0:T(8,128)S(1)}, f32[96,8,128]{2,1,0:T(8,128)}, u32[]{:S(2)}) copy-start(f32[96,8,128]{2,1,0:T(8,128)} %copy-done.3) | copy-start | bytes 1179652
  274.0 67.3 %copy-start.13 = (f32[96,8,128]{2,1,0:T(8,128)S(1)}, f32[96,8,128]{2,1,0:T(8,128)}, u32[]{:S(2)}) copy-start(f32[96,8,128]{2,1,0:T(8,128)} %copy-done.9) | copy-start | bytes 1179652
  274.0 67.3 %copy-start.19 = (f32[96,8,128]{2,1,0:T(8,128)S(1)}, f32[96,8,128]{2,1,0:T(8,128)}, u32[]{:S(2)}) copy-start(f32[96,8,128]{2,1,0:T(8,128)} %copy-done.15) | copy-start | bytes 1179652
  274.0 67.4 %copy-start.25 = (f32[96,8,128]{2,1,0:T(8,128)S(1)}, f32[96,8,128]{2,1,0:T(8,128)}, u32[]{:S(2)}) copy-start(f32[96,8,128]{2,1,0:T(8,128)} %copy-done.23) | copy-start | bytes 1179652
  351.1 42.2 %copy-start.1 = (f32[2,2,96,8,128]{4,3,2,1,0:T(8,128)}, f32[2,2,96,8,128]{4,3,2,1,0:T(8,128)S(1)}, u32[]{:S(2)}) copy-start(f32[2,2,96,8,128]{4,3,2,1,0:T(8,128)S(1)} %fusion.28) | copy-start | bytes 4718596
  353.2 7.2 %collective-permute-start.12 = (f32[2,2,96,1,128]{4,3,2,1,0:T(1,128)S(1)}, f32[2,2,96,1,128]{4,3,2,1,0:T(1,128)S(1)}, u32[]{:S(2)}, u32[]{:S(2)}) collective-permute-start(f32[2,2,96,1,128]{4,3,2,1,0:T(1,128)S(1)} %get-tuple-element.58), channel_id=1, source_target_pairs={{4,0},{8,4},{12,8},{16,12},{20,16},{24,20},{28,24},{5,1},{9,5},{13... | collective-permute-start | bytes 589832 | tf_op jit(solution)/shard_map/ppermute | solution.py:22
  355.1 7.9 %collective-permute-start.13 = (f32[2,2,96,1,128]{4,3,2,1,0:T(1,128)S(1)}, f32[2,2,96,1,128]{4,3,2,1,0:T(1,128)S(1)}, u32[]{:S(2)}, u32[]{:S(2)}) collective-permute-start(f32[2,2,96,1,128]{4,3,2,1,0:T(1,128)S(1)} %get-tuple-element.57), channel_id=1, source_target_pairs={{0,4},{4,8},{8,12},{12,16},{16,20},{20,24},{24,28},{1,5},{5,9},{9,... | collective-permute-start | bytes 589832 | tf_op jit(solution)/shard_map/ppermute | solution.py:21
  370.5 11.4 %collective-permute-start.15 = (f32[2,2,96,10,1]{2,3,4,1,0:T(8,128)S(1)}, f32[2,2,96,10,1]{2,3,4,1,0:T(8,128)S(1)}, u32[]{:S(2)}, u32[]{:S(2)}) collective-permute-start(f32[2,2,96,10,1]{2,3,4,1,0:T(8,128)S(1)} %copy.245), channel_id=1, source_target_pairs={{0,1},{1,2},{2,3},{4,5},{5,6},{6,7},{8,9},{9,10},{10,11},{12,13},{... | collective-permute-start | bytes 46088 | tf_op jit(solution)/shard_map/ppermute | solution.py:21
  375.6 8.7 %collective-permute-start.14 = (f32[2,2,96,10,1]{2,3,4,1,0:T(8,128)}, f32[2,2,96,10,1]{2,3,4,1,0:T(8,128)}, u32[]{:S(2)}, u32[]{:S(2)}) collective-permute-start(f32[2,2,96,10,1]{2,3,4,1,0:T(8,128)} %copy.243), channel_id=1, source_target_pairs={{1,0},{2,1},{3,2},{5,4},{6,5},{7,6},{9,8},{10,9},{11,10},{13,12},{... | collective-permute-start | bytes 46088 | tf_op jit(solution)/shard_map/ppermute | solution.py:22
  (27 other events, 80.8 us)
where the time goes:
time: 397 us; the launch traced here: 395 us
  blocking collectives  193 us (49%)
  local copies, waits for them, and re-layouts  70.6 us (18%)
  other arithmetic  65.2 us (16%)
  starting transfers between devices  44.3 us (11%)
  matrix products  11.9 us (3%)
  waiting for transfers between devices  8.7 us (2%)
    all_gather x3, blocking collectives, coarse_correction(): lax.all_gather(coarse_res[None], ('radial', 'axial'), axis=0, tiled=True)  193 us
    ppermute x8, starting transfers between devices, extended(): after = lax.ppermute(first, axis, down)  27.6 us
    slice x7, local copies, waits for them, and re-layouts, extended(): first = lax.slice_in_dim(shard, 0, width, axis=dim)  20 us
    add x3, other arithmetic, neighbours(): return summed + weights[4] * ahead + weights[5] * behind  18 us
    ppermute x8, starting transfers between devices, extended(): before = lax.ppermute(last, axis, up)  16.8 us
    dot_general x12, matrix products, matmul(): jnp.einsum('hij,hjk->hik', first, second, precision=lax.Precision.HIGHEST)  10.1 us
    ppermute x4, local copies, waits for them, and re-layouts, extended(): after = lax.ppermute(first, axis, down)  9.47 us
    another operation x6, other arithmetic, neighbours(): jnp.stack([jnp.concatenate([back_real, real_part[:, :-1]], 1), jnp.concat...  9.15 us
  transfers between devices with their start and end apart: 16, of which 4 were waited for; matrix products, arithmetic and copies ran while one was open for 12% of the time, Pallas kernels for 0%

commit v1 on v0

--- a/solution.py
+++ b/solution.py
@@ -9,6 +9,18 @@
 AA = 8
 LOSS_FACTOR = 0.2
 RELAXATION = 0.6
+
+
+def collect(x, axis, dim):
+    ways, here = (lax.axis_size(axis), lax.axis_index(axis))
+    grown, reach = (x, 1)
+    while reach < ways:
+        theirs = lax.ppermute(grown, axis, [(d, d ^ reach) for d in range(ways)])
+        mine_first = jnp.concatenate([grown, theirs], axis=dim)
+        theirs_first = jnp.concatenate([theirs, grown], axis=dim)
+        grown = jnp.where(here & reach == 0, mine_first, theirs_first)
+        reach = 2 * reach
+    return grown
 
 
 def extended(shard, sides, width):
@@ -125,7 +137,7 @@
     )
     radial_count = lax.axis_size("radial")
     axial_count = lax.axis_size("axial")
-    collected = lax.all_gather(coarse_res[None], ("radial", "axial"), axis=0, tiled=True)
+    collected = collect(coarse_res[None], ("radial", "axial"), 0)
     collected = collected.reshape(radial_count, axial_count, 2, shape[1], band_rows, band_cols)
     collected = collected.transpose(2, 3, 0, 4, 1, 5).reshape(
         2, shape[1], radial_count * band_rows, axial_count * band_cols

time: 397 us -> 240 us (0.60)
  blocking collectives: 193 us -> 0 us
  waiting for transfers between devices: 8.7 us -> 44.8 us
  starting transfers between devices: 44.3 us -> 49.9 us
    all_gather x3 -> x0, blocking collectives: 193 us -> none  [coarse_correction(): lax.all_gather(coarse_res[None], ('radial', 'axial'), axis=0, tiled=True)]
    ppermute x0 -> x15, waiting for transfers between devices: none -> 35.5 us  [collect(): theirs = lax.ppermute(grown, axis, [(d, d ^ reach) for d in range(ways)])]
    ppermute x0 -> x15, starting transfers between devices: none -> 6.35 us  [collect(): theirs = lax.ppermute(grown, axis, [(d, d ^ reach) for d in range(ways)])]
    unnamed x92 -> x96, local copies, waits for them, and re-layouts: 7.64 us -> 8.44 us
  transfers between devices with their start and end apart: 16 -> 31, of which waited for: 4 -> 17; matrix products, arithmetic and copies ran while one was open for 12% -> 24% of each run, Pallas kernels for 0% -> 0%
where the time goes in v1:
time: 240 us; the launch traced here: 239 us
  local copies, waits for them, and re-layouts  66.8 us (28%)
  other arithmetic  63.7 us (27%)
  starting transfers between devices  49.9 us (21%)
  waiting for transfers between devices  44.8 us (19%)
  matrix products  11.9 us (5%)
    ppermute x15, waiting for transfers between devices, collect(): theirs = lax.ppermute(grown, axis, [(d, d ^ reach) for d in range(ways)])  35.5 us
    ppermute x8, starting transfers between devices, extended(): after = lax.ppermute(first, axis, down)  25 us
    slice x7, local copies, waits for them, and re-layouts, extended(): first = lax.slice_in_dim(shard, 0, width, axis=dim)  19.9 us
    ppermute x8, starting transfers between devices, extended(): before = lax.ppermute(last, axis, up)  18.5 us
    add x3, other arithmetic, neighbours(): return summed + weights[4] * ahead + weights[5] * behind  18.1 us
    dot_general x12, matrix products, matmul(): jnp.einsum('hij,hjk->hik', first, second, precision=lax.Precision.HIGHEST)  10.1 us
    ppermute x4, local copies, waits for them, and re-layouts, extended(): after = lax.ppermute(first, axis, down)  9.38 us
    ppermute x8, waiting for transfers between devices, extended(): before = lax.ppermute(last, axis, up)  9.32 us
  transfers between devices with their start and end apart: 31, of which 17 were waited for; matrix products, arithmetic and copies ran while one was open for 24% of the time, Pallas kernels for 0%

profile of v1, /device:TPU:12, one launch (start us, length us, event | category | flops | bytes accessed | tf_op | source)
XLA Modules:
  0.0 238.8 jit_solution(2384012339527760500)
XLA Ops:
  4.4 2.8 %select_add_fusion = (f32[96,8,128]{2,0,1:T(8,128)S(1)}, pred[96,8,128]{2,0,1:T(8,128)(4,1)S(1)}, pred[96,8,128]{2,0,1:T(8,128)(4,1)S(1)}, pred[96,8,128]{2,0,1:T(8,128)(4,1)S(1)}, pred[96,8,128]{2,0,1:T(8,128)(4,1)S(1)}) fusion(f32[]{:T(128)} %bitcast.7, f32[]{:T(128)} %bitcast.6, f32[]{:T(128)} %bitcast.5, f32[]{:T(128)} %bitcast.4, ...), kind=kLoop, calls=%fused_computation.139 | loop fusion | flops 1081344 | bytes 1179664 | tf_op jit(solution)/shard_map/add | solution.py:42
  7.2 2.7 %select_add_fusion.1 = f32[96,8,128]{2,0,1:T(8,128)S(1)} fusion(pred[96,8,128]{2,0,1:T(8,128)(4,1)S(1)} %get-tuple-element.16, pred[96,8,128]{2,0,1:T(8,128)(4,1)S(1)} %get-tuple-element.15, pred[96,8,128]{2,0,1:T(8,128)(4,1)S(1)} %get-tuple-element.14, pred[96,8,128]{2,0,1:T(8,128)(4,1)S(1)} %get-tuple-element.13, f32[]{:T(128)} %bitcast.3, f32[]{:T(128)} %bitcast.2, ...), kind=kLoop, calls=%fused_computation.141 | loop fusion | flops 688128 | bytes 786448 | tf_op jit(solution)/shard_map/add | solution.py:42
  10.0 2.7 %collective-permute-start.5 = (f32[2,2,2,2,16]{4,3,2,1,0:T(2,128)S(1)}, f32[2,2,2,2,16]{4,3,2,1,0:T(2,128)S(1)}, u32[]{:S(2)}, u32[]{:S(2)}) collective-permute-start(f32[2,2,2,2,16]{4,3,2,1,0:T(2,128)S(1)} %maximum_select_fusion.12), channel_id=1, source_target_pairs={{0,2},{1,3},{2,0},{3,1},{4,6},{5,7},{6,4},{7,5},{8,10},{9,11},{10,... | collective-permute-start | bytes 3080 | tf_op jit(solution)/shard_map/ppermute | solution.py:18
  14.6 4.5 %collective-permute-start = (f32[96,1,128]{2,0,1:T(8,128)S(1)}, f32[96,1,128]{2,0,1:T(8,128)S(1)}, u32[]{:S(2)}, u32[]{:S(2)}) collective-permute-start(f32[96,1,128]{2,0,1:T(8,128)S(1)} %get-tuple-element.85), channel_id=1, source_target_pairs={{4,0},{8,4},{12,8},{16,12},{20,16},{24,20},{28,24},{5,1},{9,5},{13... | collective-permute-start | bytes 147464 | tf_op jit(solution)/shard_map/ppermute | solution.py:34
  21.1 3.3 %collective-permute-done.7 = f32[8,2,2,2,16]{4,3,2,1,0:T(2,128)S(1)} collective-permute-done((f32[8,2,2,2,16]{4,3,2,1,0:T(2,128)S(1)}, f32[8,2,2,2,16]{4,3,2,1,0:T(2,128)S(1)}, u32[]{:S(2)}, u32[]{:S(2)}) %collective-permute-start.7) | collective-permute-done | bytes 4128 | tf_op jit(solution)/shard_map/ppermute | solution.py:18
  24.9 3.9 %collective-permute-done.8 = f32[16,2,2,2,16]{4,3,2,1,0:T(2,128)S(1)} collective-permute-done((f32[16,2,2,2,16]{4,3,2,1,0:T(2,128)S(1)}, f32[16,2,2,2,16]{4,3,2,1,0:T(2,128)S(1)}, u32[]{:S(2)}, u32[]{:S(2)}) %collective-permute-start.8) | collective-permute-done | bytes 8224 | tf_op jit(solution)/shard_map/ppermute | solution.py:18
  33.6 3.5 %collective-permute-start.2 = (f32[96,10,1]{0,1,2:T(8,128)S(1)}, f32[96,10,1]{0,1,2:T(8,128)S(1)}, u32[]{:S(2)}, u32[]{:S(2)}) collective-permute-start(f32[96,10,1]{0,1,2:T(8,128)S(1)} %copy.223), channel_id=1, source_target_pairs={{1,0},{2,1},{3,2},{5,4},{6,5},{7,6},{9,8},{10,9},{11,10},{13,12},{... | collective-permute-start | bytes 11528 | tf_op jit(solution)/shard_map/ppermute | solution.py:34
  40.3 2.6 %collective-permute-done.3 = f32[96,10,1]{0,1,2:T(8,128)S(1)} collective-permute-done((f32[96,10,1]{0,1,2:T(8,128)S(1)}, f32[96,10,1]{0,1,2:T(8,128)S(1)}, u32[]{:S(2)}, u32[]{:S(2)}) %collective-permute-start.3) | collective-permute-done | bytes 3872 | tf_op jit(solution)/shard_map/ppermute | solution.py:33
  59.9 3.6 %fusion.83 = (f32[2,2,96,10,1]{4,3,2,1,0:T(8,128)}, f32[2,2,96,10,1]{4,3,2,1,0:T(8,128)}) fusion(f32[2,2,96,10,128]{4,3,2,1,0:T(8,128)S(1)} %pad_maximum_fusion), kind=kLoop, calls=%fused_computation.216 | loop fusion | bytes 61440 | tf_op jit(solution)/shard_map/slice | solution.py:32
  68.2 2.9 %copy.196 = f32[2,2,96,10,1]{2,1,4,3,0:T(2,128)} copy(f32[2,2,96,10,1]{4,3,2,1,0:T(8,128)} %get-tuple-element.41) | data formatting | bytes 30720 | tf_op jit(solution)/shard_map/slice | solution.py:32
  71.2 3.8 %collective-permute-start.11 = (f32[2,2,96,10,1]{2,1,4,3,0:T(2,128)}, f32[2,2,96,10,1]{2,1,4,3,0:T(2,128)}, u32[]{:S(2)}, u32[]{:S(2)}) collective-permute-start(f32[2,2,96,10,1]{2,1,4,3,0:T(2,128)} %copy.196), channel_id=1, source_target_pairs={{1,0},{2,1},{3,2},{5,4},{6,5},{7,6},{9,8},{10,9},{11,10},{13,12},{... | collective-permute-start | bytes 46088 | tf_op jit(solution)/shard_map/ppermute | solution.py:34
  85.5 3.0 %copy.197 = f32[2,2,96,10,1]{4,3,2,1,0:T(8,128)} copy(f32[2,2,96,10,1]{2,1,4,3,0:T(2,128)} %collective-permute-done.11) | data formatting | bytes 30720 | tf_op jit(solution)/shard_map/ppermute | solution.py:34
  88.5 6.0 %fusion.21 = f32[2,2,96,8,128]{4,3,2,1,0:T(8,128)S(1)} fusion(f32[2,2,96,10,1]{4,3,2,1,0:T(8,128)} %copy.200, f32[2,2,96,1,128]{4,3,2,1,0:T(1,128)S(1)} %collective-permute-done.9, f32[2,2,96,8,128]{4,3,2,1,0:T(8,128)S(1)} %maximum_add_fusion, f32[2,2,96,1,128]{4,3,2,1,0:T(1,128)} %copy-done.32, f32[2,2,96,10,1]{4,3,2,1,0:T(8,128)} %copy.197, ...), kind=kLoop, calls=%fused_computation.41 | loop fusion | flops 8257536 | bytes 9074688 | tf_op jit(solution)/shard_map/add | solution.py:82
  99.2 3.6 %collective-permute-done.13 = f32[1,2,2,2,16]{4,3,2,1,0:T(2,128)S(1)} collective-permute-done((f32[1,2,2,2,16]{4,3,2,1,0:T(2,128)S(1)}, f32[1,2,2,2,16]{4,3,2,1,0:T(2,128)S(1)}, u32[]{:S(2)}, u32[]{:S(2)}) %collective-permute-start.13) | collective-permute-done | bytes 544 | tf_op jit(solution)/shard_map/ppermute | solution.py:18
  103.6 3.8 %collective-permute-done.14 = f32[2,2,2,2,16]{4,3,2,1,0:T(2,128)S(1)} collective-permute-done((f32[2,2,2,2,16]{4,3,2,1,0:T(2,128)S(1)}, f32[2,2,2,2,16]{4,3,2,1,0:T(2,128)S(1)}, u32[]{:S(2)}, u32[]{:S(2)}) %collective-permute-start.14) | collective-permute-done | bytes 1056 | tf_op jit(solution)/shard_map/ppermute | solution.py:18
  108.8 3.9 %collective-permute-done.16 = f32[8,2,2,2,16]{4,3,2,1,0:T(2,128)S(1)} collective-permute-done((f32[8,2,2,2,16]{4,3,2,1,0:T(2,128)S(1)}, f32[8,2,2,2,16]{4,3,2,1,0:T(2,128)S(1)}, u32[]{:S(2)}, u32[]{:S(2)}) %collective-permute-start.16) | collective-permute-done | bytes 4128 | tf_op jit(solution)/shard_map/ppermute | solution.py:18
  112.9 3.0 %add_multiply_fusion.1 = (f32[1,2,96,8,128]{4,3,2,1,0:T(8,128)}, f32[1,2,96,8,128]{4,3,2,1,0:T(8,128)}) fusion(f32[2,2,96,8,128]{4,3,2,1,0:T(8,128)} %get-tuple-element.11, f32[96,8,128]{2,1,0:T(8,128)S(1)} %copy-done.24, f32[96,8,128]{2,1,0:T(8,128)S(1)} %copy-done.17, f32[96,8,128]{2,1,0:T(8,128)S(1)} %copy-done.5, f32[2]{0:T(128)S(1)} %copy-done.36, ...), kind=kLoop, calls=%fused_computation.105 | loop fusion | flops 2555904 | bytes 4718600 | tf_op jit(solution)/shard_map/mul | solution.py:121
  132.4 2.7 %collective-permute-done.19 = f32[2,2,96,1,128]{4,3,2,1,0:T(1,128)S(1)} collective-permute-done((f32[2,2,96,1,128]{4,3,2,1,0:T(1,128)S(1)}, f32[2,2,96,1,128]{4,3,2,1,0:T(1,128)S(1)}, u32[]{:S(2)}, u32[]{:S(2)}) %collective-permute-start.19) | collective-permute-done | bytes 196640 | tf_op jit(solution)/shard_map/ppermute | solution.py:33
  136.4 3.6 %fusion.82 = (f32[2,2,96,10,1]{4,3,2,1,0:T(8,128)}, f32[2,2,96,10,1]{4,3,2,1,0:T(8,128)}) fusion(f32[2,2,96,10,128]{4,3,2,1,0:T(8,128)S(1)} %pad_maximum_fusion.1), kind=kLoop, calls=%fused_computation.215 | loop fusion | bytes 61440 | tf_op jit(solution)/shard_map/slice | solution.py:32
  144.7 3.0 %copy.206 = f32[2,2,96,10,1]{2,1,4,3,0:T(2,128)} copy(f32[2,2,96,10,1]{4,3,2,1,0:T(8,128)} %get-tuple-element.39) | data formatting | bytes 30720 | tf_op jit(solution)/shard_map/slice | solution.py:32
  147.6 3.7 %collective-permute-start.20 = (f32[2,2,96,10,1]{2,1,4,3,0:T(2,128)}, f32[2,2,96,10,1]{2,1,4,3,0:T(2,128)}, u32[]{:S(2)}, u32[]{:S(2)}) collective-permute-start(f32[2,2,96,10,1]{2,1,4,3,0:T(2,128)} %copy.206), channel_id=1, source_target_pairs={{1,0},{2,1},{3,2},{5,4},{6,5},{7,6},{9,8},{10,9},{11,10},{13,12},{... | collective-permute-start | bytes 46088 | tf_op jit(solution)/shard_map/ppermute | solution.py:34
  155.7 3.0 %copy.207 = f32[2,2,96,10,1]{4,3,2,1,0:T(8,128)} copy(f32[2,2,96,10,1]{2,1,4,3,0:T(2,128)} %collective-permute-done.20) | data formatting | bytes 30720 | tf_op jit(solution)/shard_map/ppermute | solution.py:34
  158.8 6.0 %fusion.12 = f32[2,2,96,8,128]{4,3,2,1,0:T(8,128)S(1)} fusion(f32[2,2,96,10,1]{4,3,2,1,0:T(8,128)} %copy.209, f32[2,2,96,1,128]{4,3,2,1,0:T(1,128)S(1)} %collective-permute-done.18, f32[2,2,96,8,128]{4,3,2,1,0:T(8,128)S(1)} %fusion.27, f32[2,2,96,1,128]{4,3,2,1,0:T(1,128)} %copy-done.34, f32[2,2,96,10,1]{4,3,2,1,0:T(8,128)} %copy.207, ...), kind=kLoop, calls=%fused_computation.24 | loop fusion | flops 8257536 | bytes 9074688 | tf_op jit(solution)/shard_map/add | solution.py:82
  169.5 3.6 %collective-permute-done.22 = f32[1,2,2,2,16]{4,3,2,1,0:T(2,128)S(1)} collective-permute-done((f32[1,2,2,2,16]{4,3,2,1,0:T(2,128)S(1)}, f32[1,2,2,2,16]{4,3,2,1,0:T(2,128)S(1)}, u32[]{:S(2)}, u32[]{:S(2)}) %collective-permute-start.22) | collective-permute-done | bytes 544 | tf_op jit(solution)/shard_map/ppermute | solution.py:18
  174.3 3.5 %collective-permute-done.23 = f32[2,2,2,2,16]{4,3,2,1,0:T(2,128)S(1)} collective-permute-done((f32[2,2,2,2,16]{4,3,2,1,0:T(2,128)S(1)}, f32[2,2,2,2,16]{4,3,2,1,0:T(2,128)S(1)}, u32[]{:S(2)}, u32[]{:S(2)}) %collective-permute-start.23) | collective-permute-done | bytes 1056 | tf_op jit(solution)/shard_map/ppermute | solution.py:18
  179.1 3.9 %collective-permute-done.25 = f32[8,2,2,2,16]{4,3,2,1,0:T(2,128)S(1)} collective-permute-done((f32[8,2,2,2,16]{4,3,2,1,0:T(2,128)S(1)}, f32[8,2,2,2,16]{4,3,2,1,0:T(2,128)S(1)}, u32[]{:S(2)}, u32[]{:S(2)}) %collective-permute-start.25) | collective-permute-done | bytes 4128 | tf_op jit(solution)/shard_map/ppermute | solution.py:18
  183.2 2.9 %add_multiply_fusion = (f32[1,2,96,8,128]{4,3,2,1,0:T(8,128)}, f32[1,2,96,8,128]{4,3,2,1,0:T(8,128)}) fusion(f32[2,2,96,8,128]{4,3,2,1,0:T(8,128)} %get-tuple-element.9, f32[96,8,128]{2,1,0:T(8,128)S(1)} %copy-done.25, f32[96,8,128]{2,1,0:T(8,128)S(1)} %copy-done.19, f32[96,8,128]{2,1,0:T(8,128)S(1)} %copy-done.7, f32[2]{0:T(128)S(1)} %copy-done.37, ...), kind=kLoop, calls=%fused_computation.101 | loop fusion | flops 2555904 | bytes 4718600 | tf_op jit(solution)/shard_map/mul | solution.py:121
  207.8 3.6 %fusion.81 = (f32[2,2,96,10,1]{4,3,2,1,0:T(8,128)}, f32[2,2,96,10,1]{4,3,2,1,0:T(8,128)}) fusion(f32[2,2,96,10,128]{4,3,2,1,0:T(8,128)S(1)} %pad_maximum_fusion.2), kind=kLoop, calls=%fused_computation.214 | loop fusion | bytes 61440 | tf_op jit(solution)/shard_map/slice | solution.py:32
  216.4 3.2 %copy.213 = f32[2,2,96,10,1]{2,3,4,1,0:T(8,128)} copy(f32[2,2,96,10,1]{4,3,2,1,0:T(8,128)} %get-tuple-element.37) | data formatting | bytes 30720 | tf_op jit(solution)/shard_map/slice | solution.py:32
  219.6 3.7 %collective-permute-start.29 = (f32[2,2,96,10,1]{2,3,4,1,0:T(8,128)}, f32[2,2,96,10,1]{2,3,4,1,0:T(8,128)}, u32[]{:S(2)}, u32[]{:S(2)}) collective-permute-start(f32[2,2,96,10,1]{2,3,4,1,0:T(8,128)} %copy.213), channel_id=1, source_target_pairs={{1,0},{2,1},{3,2},{5,4},{6,5},{7,6},{9,8},{10,9},{11,10},{13,12},{... | collective-permute-start | bytes 46088 | tf_op jit(solution)/shard_map/ppermute | solution.py:34
  227.7 3.1 %copy.214 = f32[2,2,96,10,1]{4,3,2,1,0:T(8,128)} copy(f32[2,2,96,10,1]{2,3,4,1,0:T(8,128)} %collective-permute-done.29) | data formatting | bytes 30720 | tf_op jit(solution)/shard_map/ppermute | solution.py:34
  230.8 6.2 %fusion.3 = f32[2,2,96,8,128]{4,3,2,1,0:T(8,128)S(1)} fusion(f32[2,2,96,10,1]{4,3,2,1,0:T(8,128)} %copy.216, f32[2,2,96,1,128]{4,3,2,1,0:T(1,128)S(1)} %collective-permute-done.27, f32[2,2,96,8,128]{4,3,2,1,0:T(8,128)S(1)} %fusion.28, f32[2,2,96,1,128]{4,3,2,1,0:T(1,128)} %copy-done.33, f32[2,2,96,10,1]{4,3,2,1,0:T(8,128)} %copy.214, ...), kind=kLoop, calls=%fused_computation.7 | loop fusion | flops 8257536 | bytes 9074688 | tf_op jit(solution)/shard_map/add | solution.py:82
  (277 shorter events, 121.8 us)
Async XLA Ops:
  2.5 7.4 %collective-permute-start.4 = (f32[1,2,2,2,16]{4,3,2,1,0:T(2,128)S(1)}, f32[1,2,2,2,16]{4,3,2,1,0:T(2,128)S(1)}, u32[]{:S(2)}, u32[]{:S(2)}) collective-permute-start(f32[1,2,2,2,16]{4,3,2,1,0:T(2,128)S(1)} %bitcast.151), channel_id=1, source_target_pairs={{0,1},{1,0},{2,3},{3,2},{4,5},{5,4},{6,7},{7,6},{8,9},{9,8},{10,11... | collective-permute-start | bytes 1544 | tf_op jit(solution)/shard_map/ppermute | solution.py:18
  10.0 9.1 %collective-permute-start.5 = (f32[2,2,2,2,16]{4,3,2,1,0:T(2,128)S(1)}, f32[2,2,2,2,16]{4,3,2,1,0:T(2,128)S(1)}, u32[]{:S(2)}, u32[]{:S(2)}) collective-permute-start(f32[2,2,2,2,16]{4,3,2,1,0:T(2,128)S(1)} %maximum_select_fusion.12), channel_id=1, source_target_pairs={{0,2},{1,3},{2,0},{3,1},{4,6},{5,7},{6,4},{7,5},{8,10},{9,11},{10,... | collective-permute-start | bytes 3080 | tf_op jit(solution)/shard_map/ppermute | solution.py:18
  12.6 20.5 %collective-permute-start.1 = (f32[96,1,128]{2,0,1:T(8,128)S(1)}, f32[96,1,128]{2,0,1:T(8,128)S(1)}, u32[]{:S(2)}, u32[]{:S(2)}) collective-permute-start(f32[96,1,128]{2,0,1:T(8,128)S(1)} %get-tuple-element.86), channel_id=1, source_target_pairs={{0,4},{4,8},{8,12},{12,16},{16,20},{20,24},{24,28},{1,5},{5,9},{9,... | collective-permute-start | bytes 147464 | tf_op jit(solution)/shard_map/ppermute | solution.py:33
  14.6 18.5 %collective-permute-start = (f32[96,1,128]{2,0,1:T(8,128)S(1)}, f32[96,1,128]{2,0,1:T(8,128)S(1)}, u32[]{:S(2)}, u32[]{:S(2)}) collective-permute-start(f32[96,1,128]{2,0,1:T(8,128)S(1)} %get-tuple-element.85), channel_id=1, source_target_pairs={{4,0},{8,4},{12,8},{16,12},{20,16},{24,20},{28,24},{5,1},{9,5},{13... | collective-permute-start | bytes 147464 | tf_op jit(solution)/shard_map/ppermute | solution.py:34
  19.1 1.2 collective-permute-start.6
  20.4 4.0 %collective-permute-start.7 = (f32[8,2,2,2,16]{4,3,2,1,0:T(2,128)S(1)}, f32[8,2,2,2,16]{4,3,2,1,0:T(2,128)S(1)}, u32[]{:S(2)}, u32[]{:S(2)}) collective-permute-start(f32[8,2,2,2,16]{4,3,2,1,0:T(2,128)S(1)} %maximum_select_fusion.6), channel_id=1, source_target_pairs={{0,8},{1,9},{2,10},{3,11},{4,12},{5,13},{6,14},{7,15},{8,0},{9,1},... | collective-permute-start | bytes 12296 | tf_op jit(solution)/shard_map/ppermute | solution.py:18
  24.4 4.3 %collective-permute-start.8 = (f32[16,2,2,2,16]{4,3,2,1,0:T(2,128)S(1)}, f32[16,2,2,2,16]{4,3,2,1,0:T(2,128)S(1)}, u32[]{:S(2)}, u32[]{:S(2)}) collective-permute-start(f32[16,2,2,2,16]{4,3,2,1,0:T(2,128)S(1)} %maximum_select_fusion.3), channel_id=1, source_target_pairs={{0,16},{1,17},{2,18},{3,19},{4,20},{5,21},{6,22},{7,23},{8,24},{9,... | collective-permute-start | bytes 24584 | tf_op jit(solution)/shard_map/ppermute | solution.py:18
  24.6 99.6 %copy-start.42 = (f32[2]{0:T(128)}, f32[2]{0:T(128)S(1)}, u32[]{:S(2)}) copy-start(f32[2]{0:T(128)S(1)} %get-tuple-element.94) | copy-start | bytes 28
  33.6 6.4 %collective-permute-start.2 = (f32[96,10,1]{0,1,2:T(8,128)S(1)}, f32[96,10,1]{0,1,2:T(8,128)S(1)}, u32[]{:S(2)}, u32[]{:S(2)}) collective-permute-start(f32[96,10,1]{0,1,2:T(8,128)S(1)} %copy.223), channel_id=1, source_target_pairs={{1,0},{2,1},{3,2},{5,4},{6,5},{7,6},{9,8},{10,9},{11,10},{13,12},{... | collective-permute-start | bytes 11528 | tf_op jit(solution)/shard_map/ppermute | solution.py:34
  37.4 5.5 %collective-permute-start.3 = (f32[96,10,1]{0,1,2:T(8,128)S(1)}, f32[96,10,1]{0,1,2:T(8,128)S(1)}, u32[]{:S(2)}, u32[]{:S(2)}) collective-permute-start(f32[96,10,1]{0,1,2:T(8,128)S(1)} %copy.224), channel_id=1, source_target_pairs={{0,1},{1,2},{2,3},{4,5},{5,6},{6,7},{8,9},{9,10},{10,11},{12,13},{... | collective-permute-start | bytes 11528 | tf_op jit(solution)/shard_map/ppermute | solution.py:33
  48.9 8.3 %collective-permute-start.9 = (f32[2,2,96,1,128]{4,3,2,1,0:T(1,128)S(1)}, f32[2,2,96,1,128]{4,3,2,1,0:T(1,128)S(1)}, u32[]{:S(2)}, u32[]{:S(2)}) collective-permute-start(f32[2,2,96,1,128]{4,3,2,1,0:T(1,128)S(1)} %get-tuple-element.66), channel_id=1, source_target_pairs={{4,0},{8,4},{12,8},{16,12},{20,16},{24,20},{28,24},{5,1},{9,5},{13... | collective-permute-start | bytes 589832 | tf_op jit(solution)/shard_map/ppermute | solution.py:34
  50.8 7.9 %collective-permute-start.10 = (f32[2,2,96,1,128]{4,3,2,1,0:T(1,128)S(1)}, f32[2,2,96,1,128]{4,3,2,1,0:T(1,128)S(1)}, u32[]{:S(2)}, u32[]{:S(2)}) collective-permute-start(f32[2,2,96,1,128]{4,3,2,1,0:T(1,128)S(1)} %get-tuple-element.65), channel_id=1, source_target_pairs={{0,4},{4,8},{8,12},{12,16},{16,20},{20,24},{24,28},{1,5},{5,9},{9,... | collective-permute-start | bytes 589832 | tf_op jit(solution)/shard_map/ppermute | solution.py:33
  65.9 17.2 %collective-permute-start.12 = (f32[2,2,96,10,1]{2,1,4,3,0:T(2,128)S(1)}, f32[2,2,96,10,1]{2,1,4,3,0:T(2,128)S(1)}, u32[]{:S(2)}, u32[]{:S(2)}) collective-permute-start(f32[2,2,96,10,1]{2,1,4,3,0:T(2,128)S(1)} %copy.199), channel_id=1, source_target_pairs={{0,1},{1,2},{2,3},{4,5},{5,6},{6,7},{8,9},{9,10},{10,11},{12,13},{... | collective-permute-start | bytes 46088 | tf_op jit(solution)/shard_map/ppermute | solution.py:33
  71.2 14.3 %collective-permute-start.11 = (f32[2,2,96,10,1]{2,1,4,3,0:T(2,128)}, f32[2,2,96,10,1]{2,1,4,3,0:T(2,128)}, u32[]{:S(2)}, u32[]{:S(2)}) collective-permute-start(f32[2,2,96,10,1]{2,1,4,3,0:T(2,128)} %copy.196), channel_id=1, source_target_pairs={{1,0},{2,1},{3,2},{5,4},{6,5},{7,6},{9,8},{10,9},{11,10},{13,12},{... | collective-permute-start | bytes 46088 | tf_op jit(solution)/shard_map/ppermute | solution.py:34
  99.2 3.6 %collective-permute-start.13 = (f32[1,2,2,2,16]{4,3,2,1,0:T(2,128)S(1)}, f32[1,2,2,2,16]{4,3,2,1,0:T(2,128)S(1)}, u32[]{:S(2)}, u32[]{:S(2)}) collective-permute-start(f32[1,2,2,2,16]{4,3,2,1,0:T(2,128)S(1)} %bitcast.155), channel_id=1, source_target_pairs={{0,1},{1,0},{2,3},{3,2},{4,5},{5,4},{6,7},{7,6},{8,9},{9,8},{10,11... | collective-permute-start | bytes 1544 | tf_op jit(solution)/shard_map/ppermute | solution.py:18
  102.8 4.6 %collective-permute-start.14 = (f32[2,2,2,2,16]{4,3,2,1,0:T(2,128)S(1)}, f32[2,2,2,2,16]{4,3,2,1,0:T(2,128)S(1)}, u32[]{:S(2)}, u32[]{:S(2)}) collective-permute-start(f32[2,2,2,2,16]{4,3,2,1,0:T(2,128)S(1)} %maximum_select_fusion.13), channel_id=1, source_target_pairs={{0,2},{1,3},{2,0},{3,1},{4,6},{5,7},{6,4},{7,5},{8,10},{9,11},{10,... | collective-permute-start | bytes 3080 | tf_op jit(solution)/shard_map/ppermute | solution.py:18
  107.4 1.2 collective-permute-start.15
  108.7 4.0 %collective-permute-start.16 = (f32[8,2,2,2,16]{4,3,2,1,0:T(2,128)S(1)}, f32[8,2,2,2,16]{4,3,2,1,0:T(2,128)S(1)}, u32[]{:S(2)}, u32[]{:S(2)}) collective-permute-start(f32[8,2,2,2,16]{4,3,2,1,0:T(2,128)S(1)} %maximum_select_fusion.7), channel_id=1, source_target_pairs={{0,8},{1,9},{2,10},{3,11},{4,12},{5,13},{6,14},{7,15},{8,0},{9,1},... | collective-permute-start | bytes 12296 | tf_op jit(solution)/shard_map/ppermute | solution.py:18
  112.7 4.3 %collective-permute-start.17 = (f32[16,2,2,2,16]{4,3,2,1,0:T(2,128)S(1)}, f32[16,2,2,2,16]{4,3,2,1,0:T(2,128)S(1)}, u32[]{:S(2)}, u32[]{:S(2)}) collective-permute-start(f32[16,2,2,2,16]{4,3,2,1,0:T(2,128)S(1)} %maximum_select_fusion.4), channel_id=1, source_target_pairs={{0,16},{1,17},{2,18},{3,19},{4,20},{5,21},{6,22},{7,23},{8,24},{9,... | collective-permute-start | bytes 24584 | tf_op jit(solution)/shard_map/ppermute | solution.py:18
  125.3 7.2 %collective-permute-start.18 = (f32[2,2,96,1,128]{4,3,2,1,0:T(1,128)S(1)}, f32[2,2,96,1,128]{4,3,2,1,0:T(1,128)S(1)}, u32[]{:S(2)}, u32[]{:S(2)}) collective-permute-start(f32[2,2,96,1,128]{4,3,2,1,0:T(1,128)S(1)} %get-tuple-element.62), channel_id=1, source_target_pairs={{4,0},{8,4},{12,8},{16,12},{20,16},{24,20},{28,24},{5,1},{9,5},{13... | collective-permute-start | bytes 589832 | tf_op jit(solution)/shard_map/ppermute | solution.py:34
  127.2 7.9 %collective-permute-start.19 = (f32[2,2,96,1,128]{4,3,2,1,0:T(1,128)S(1)}, f32[2,2,96,1,128]{4,3,2,1,0:T(1,128)S(1)}, u32[]{:S(2)}, u32[]{:S(2)}) collective-permute-start(f32[2,2,96,1,128]{4,3,2,1,0:T(1,128)S(1)} %get-tuple-element.61), channel_id=1, source_target_pairs={{0,4},{4,8},{8,12},{12,16},{16,20},{20,24},{24,28},{1,5},{5,9},{9,... | collective-permute-start | bytes 589832 | tf_op jit(solution)/shard_map/ppermute | solution.py:33
  142.3 11.1 %collective-permute-start.21 = (f32[2,2,96,10,1]{2,1,4,3,0:T(2,128)S(1)}, f32[2,2,96,10,1]{2,1,4,3,0:T(2,128)S(1)}, u32[]{:S(2)}, u32[]{:S(2)}) collective-permute-start(f32[2,2,96,10,1]{2,1,4,3,0:T(2,128)S(1)} %copy.208), channel_id=1, source_target_pairs={{0,1},{1,2},{2,3},{4,5},{5,6},{6,7},{8,9},{9,10},{10,11},{12,13},{... | collective-permute-start | bytes 46088 | tf_op jit(solution)/shard_map/ppermute | solution.py:33
  147.6 8.1 %collective-permute-start.20 = (f32[2,2,96,10,1]{2,1,4,3,0:T(2,128)}, f32[2,2,96,10,1]{2,1,4,3,0:T(2,128)}, u32[]{:S(2)}, u32[]{:S(2)}) collective-permute-start(f32[2,2,96,10,1]{2,1,4,3,0:T(2,128)} %copy.206), channel_id=1, source_target_pairs={{1,0},{2,1},{3,2},{5,4},{6,5},{7,6},{9,8},{10,9},{11,10},{13,12},{... | collective-permute-start | bytes 46088 | tf_op jit(solution)/shard_map/ppermute | solution.py:34
  169.5 3.6 %collective-permute-start.22 = (f32[1,2,2,2,16]{4,3,2,1,0:T(2,128)S(1)}, f32[1,2,2,2,16]{4,3,2,1,0:T(2,128)S(1)}, u32[]{:S(2)}, u32[]{:S(2)}) collective-permute-start(f32[1,2,2,2,16]{4,3,2,1,0:T(2,128)S(1)} %bitcast.153), channel_id=1, source_target_pairs={{0,1},{1,0},{2,3},{3,2},{4,5},{5,4},{6,7},{7,6},{8,9},{9,8},{10,11... | collective-permute-start | bytes 1544 | tf_op jit(solution)/shard_map/ppermute | solution.py:18
  173.1 4.6 %collective-permute-start.23 = (f32[2,2,2,2,16]{4,3,2,1,0:T(2,128)S(1)}, f32[2,2,2,2,16]{4,3,2,1,0:T(2,128)S(1)}, u32[]{:S(2)}, u32[]{:S(2)}) collective-permute-start(f32[2,2,2,2,16]{4,3,2,1,0:T(2,128)S(1)} %maximum_select_fusion.14), channel_id=1, source_target_pairs={{0,2},{1,3},{2,0},{3,1},{4,6},{5,7},{6,4},{7,5},{8,10},{9,11},{10,... | collective-permute-start | bytes 3080 | tf_op jit(solution)/shard_map/ppermute | solution.py:18
  177.7 1.2 collective-permute-start.24
  179.0 4.0 %collective-permute-start.25 = (f32[8,2,2,2,16]{4,3,2,1,0:T(2,128)S(1)}, f32[8,2,2,2,16]{4,3,2,1,0:T(2,128)S(1)}, u32[]{:S(2)}, u32[]{:S(2)}) collective-permute-start(f32[8,2,2,2,16]{4,3,2,1,0:T(2,128)S(1)} %maximum_select_fusion.8), channel_id=1, source_target_pairs={{0,8},{1,9},{2,10},{3,11},{4,12},{5,13},{6,14},{7,15},{8,0},{9,1},... | collective-permute-start | bytes 12296 | tf_op jit(solution)/shard_map/ppermute | solution.py:18
  183.0 4.3 %collective-permute-start.26 = (f32[16,2,2,2,16]{4,3,2,1,0:T(2,128)S(1)}, f32[16,2,2,2,16]{4,3,2,1,0:T(2,128)S(1)}, u32[]{:S(2)}, u32[]{:S(2)}) collective-permute-start(f32[16,2,2,2,16]{4,3,2,1,0:T(2,128)S(1)} %maximum_select_fusion.5), channel_id=1, source_target_pairs={{0,16},{1,17},{2,18},{3,19},{4,20},{5,21},{6,22},{7,23},{8,24},{9,... | collective-permute-start | bytes 24584 | tf_op jit(solution)/shard_map/ppermute | solution.py:18
  196.7 7.3 %collective-permute-start.27 = (f32[2,2,96,1,128]{4,3,2,1,0:T(1,128)S(1)}, f32[2,2,96,1,128]{4,3,2,1,0:T(1,128)S(1)}, u32[]{:S(2)}, u32[]{:S(2)}) collective-permute-start(f32[2,2,96,1,128]{4,3,2,1,0:T(1,128)S(1)} %get-tuple-element.58), channel_id=1, source_target_pairs={{4,0},{8,4},{12,8},{16,12},{20,16},{24,20},{28,24},{5,1},{9,5},{13... | collective-permute-start | bytes 589832 | tf_op jit(solution)/shard_map/ppermute | solution.py:34
  198.6 7.9 %collective-permute-start.28 = (f32[2,2,96,1,128]{4,3,2,1,0:T(1,128)S(1)}, f32[2,2,96,1,128]{4,3,2,1,0:T(1,128)S(1)}, u32[]{:S(2)}, u32[]{:S(2)}) collective-permute-start(f32[2,2,96,1,128]{4,3,2,1,0:T(1,128)S(1)} %get-tuple-element.57), channel_id=1, source_target_pairs={{0,4},{4,8},{8,12},{12,16},{16,20},{20,24},{24,28},{1,5},{5,9},{9,... | collective-permute-start | bytes 589832 | tf_op jit(solution)/shard_map/ppermute | solution.py:33
  214.0 11.3 %collective-permute-start.30 = (f32[2,2,96,10,1]{2,3,4,1,0:T(8,128)S(1)}, f32[2,2,96,10,1]{2,3,4,1,0:T(8,128)S(1)}, u32[]{:S(2)}, u32[]{:S(2)}) collective-permute-start(f32[2,2,96,10,1]{2,3,4,1,0:T(8,128)S(1)} %copy.215), channel_id=1, source_target_pairs={{0,1},{1,2},{2,3},{4,5},{5,6},{6,7},{8,9},{9,10},{10,11},{12,13},{... | collective-permute-start | bytes 46088 | tf_op jit(solution)/shard_map/ppermute | solution.py:33
  219.6 8.2 %collective-permute-start.29 = (f32[2,2,96,10,1]{2,3,4,1,0:T(8,128)}, f32[2,2,96,10,1]{2,3,4,1,0:T(8,128)}, u32[]{:S(2)}, u32[]{:S(2)}) collective-permute-start(f32[2,2,96,10,1]{2,3,4,1,0:T(8,128)} %copy.213), channel_id=1, source_target_pairs={{1,0},{2,1},{3,2},{5,4},{6,5},{7,6},{9,8},{10,9},{11,10},{13,12},{... | collective-permute-start | bytes 46088 | tf_op jit(solution)/shard_map/ppermute | solution.py:34
  (44 other events, 451.1 us)
